TPU v7x, 32 devices: a whole 2x2x4 slice. The times are simulated.
32 devices in a mesh: ch: 8 (over y, x, core), ta: 4 (over z).
Axes of the slice: x: 2, y: 2, z: 4, core: 2. Of those that a mesh axis runs over, the one named last changes fastest.
Arguments:
- raw: bfloat16 [2048, 20480], P('ch', 'ta'), may hold values from -40 to 40
- fir_taps: bfloat16 [129], replicated, may hold values from -0.5 to 0.5
- start_basis: float32 [512, 16], replicated, may hold values from -6 to 6
Outputs:
- cleaned: bfloat16 [2048, 20480], P('ch', 'ta')
All inputs are finite; a program needn't handle non-finite values.
Results may differ from a plain program's by a relative error of at most 0.008.
Values may be sent and summed in bfloat16 or wider, within the bound.
A program may use at most 64 MiB of HBM per device.

v0:
```python
import math

import jax
import jax.numpy as jnp
from jax import lax
from jax.sharding import PartitionSpec as P

TAPS = 129
GAUGE = 4
STRIDE = 128
RANK = 16
ITERS = 6
WIN = 512


def with_halo(block, sides, width):
    for axis, dim in sides:
        count = lax.axis_size(axis)
        forward = [(i, i + 1) for i in range(count - 1)]
        backward = [(target, source) for source, target in forward]
        low = lax.ppermute(
            lax.slice_in_dim(block, block.shape[dim] - width, None, axis=dim), axis, forward
        )
        high = lax.ppermute(lax.slice_in_dim(block, 0, width, axis=dim), axis, backward)
        block = jnp.concatenate([low, block, high], axis=dim)
    return block


def shifted(value, axis, steps):
    count = lax.axis_size(axis)
    first, last = (max(0, -steps), min(count, count - steps))
    return lax.ppermute(value, axis, [(source, source + steps) for source in range(first, last)])


def toeplitz_band(taps, width):
    count = taps.shape[0]
    line = jnp.concatenate([taps, jnp.zeros((width,), taps.dtype)])
    flat = jnp.tile(line, width)[: width * (count + width - 1)]
    return flat.reshape(width, count + width - 1).T


def orthonormal(image):
    gram = jnp.einsum("wcr,wcs->wrs", image, image, precision=lax.Precision.HIGHEST)
    lower = jnp.linalg.cholesky(gram)
    return lax.linalg.triangular_solve(lower, image, left_side=False, lower=True, transpose_a=True)


def per_device(raw, fir_taps, start_basis):
    chans = raw.shape[0]
    samples = raw.shape[1]
    half = (TAPS - 1) // 2
    width = math.gcd(samples, 256)
    padded = with_halo(raw, (("ta", 1),), half)
    band_matrix = toeplitz_band(fir_taps, width)
    pieces = jnp.stack(
        [
            padded[:, number * width : number * width + width + TAPS - 1]
            for number in range(samples // width)
        ]
    )
    filtered = jnp.einsum(
        "bct,tu->cbu", pieces, band_matrix, preferred_element_type=jnp.float32
    ).reshape(chans, samples)
    extended = with_halo(filtered, (("ch", 0),), GAUGE)
    gauged = (extended[2 * GAUGE :] - extended[: -2 * GAUGE]).astype(jnp.bfloat16)
    lower_part = shifted(gauged, "ch", 1)
    upper_part = shifted(gauged[:STRIDE], "ch", -1)
    stacked = jnp.concatenate([lower_part, gauged, upper_part], axis=0)
    windows = chans // STRIDE
    total_time = samples * lax.axis_size("ta")
    basis = jnp.broadcast_to(start_basis, (windows, WIN, RANK))
    partial_mats = jnp.stack(
        [
            jnp.dot(
                stacked[number * STRIDE : number * STRIDE + WIN],
                stacked[number * STRIDE : number * STRIDE + WIN].T,
                preferred_element_type=jnp.float32,
            )
            for number in range(windows)
        ]
    )
    scatter_mat = lax.psum(partial_mats, "ta") / total_time
    for sweep in range(ITERS):
        basis = orthonormal(
            jnp.einsum("wcd,wdr->wcr", scatter_mat, basis, precision=lax.Precision.HIGHEST)
        )
    rounded = basis.astype(jnp.bfloat16)
    outputs = []
    for number in range(windows):
        frame = stacked[number * STRIDE : number * STRIDE + WIN]
        coeffs = jnp.dot(rounded[number].T, frame, preferred_element_type=jnp.float32).astype(
            jnp.bfloat16
        )
        fitted = jnp.dot(
            rounded[number, 2 * STRIDE : 3 * STRIDE], coeffs, preferred_element_type=jnp.float32
        )
        outputs.append(
            (frame[2 * STRIDE : 3 * STRIDE].astype(jnp.float32) - fitted).astype(jnp.bfloat16)
        )
    return jnp.concatenate(outputs, axis=0)


def solution(mesh):
    return jax.shard_map(
        per_device,
        mesh=mesh,
        in_specs=(P("ch", "ta"), P(), P()),
        out_specs=P("ch", "ta"),
        check_vma=False,
    )
```

profile of v0, /device:TPU:4, one launch (start us, length us, event | category | flops | bytes accessed | tf_op | source)
XLA Modules:
  0.0 257.7 jit_solution(11973980490168373167)
XLA Ops:
  6.5 1.1 fusion.57
  7.7 3.5 %collective-permute-start = (bf16[256,64]{1,0:T(8,128)(2,1)S(1)}, bf16[256,64]{1,0:T(8,128)(2,1)S(1)}, u32[]{:S(2)}, u32[]{:S(2)}) collective-permute-start(bf16[256,64]{1,0:T(8,128)(2,1)S(1)} %get-tuple-element.10), channel_id=1, source_target_pairs={{0,1},{1,2},{2,3},{4,5},{5,6},{6,7},{8,9},{9,10},{10,11},{12,13},{... | collective-permute-start | bytes 98312 | tf_op jit(solution)/shard_map/ppermute | solution.py:21
  11.1 1.3 collective-permute-start.1
  12.4 0.7 concatenate.26
  13.1 0.6 tile.10
  13.9 1.0 fusion.30
  14.9 0.1 bitcast_dynamic-update-slice_fusion.17
  15.1 0.1 bitcast_dynamic-update-slice_fusion.16
  15.2 0.1 bitcast_dynamic-update-slice_fusion.15
  15.3 0.1 bitcast_dynamic-update-slice_fusion.14
  15.5 0.1 bitcast_dynamic-update-slice_fusion.13
  15.6 0.1 bitcast_dynamic-update-slice_fusion.12
  15.8 0.1 bitcast_dynamic-update-slice_fusion.11
  15.9 0.1 bitcast_dynamic-update-slice_fusion.10
  16.0 0.1 bitcast_dynamic-update-slice_fusion.9
  16.2 0.1 bitcast_dynamic-update-slice_fusion.8
  17.4 0.2 fusion.28
  17.6 1.5 convolution_bitcast_fusion
  19.2 2.3 copy-done.3
  21.5 2.5 collective-permute-start.2
  24.0 1.9 collective-permute-start.3
  26.0 5.9 %copy.21 = f32[256,20,256]{0,2,1:T(8,128)} copy(f32[256,20,256]{2,0,1:T(8,128)} %copy-done.3) | data formatting | bytes 10485760 | tf_op jit(solution)/shard_map/bct,tu->cbu/transpose | solution.py:61
  31.9 5.9 %copy.22 = f32[256,5120]{1,0:T(8,128)} copy(f32[256,5120]{0,1:T(8,128)} %bitcast.160) | data formatting | bytes 10485760 | tf_op jit(solution)/shard_map/reshape | solution.py:63
  37.9 4.7 %fusion.3 = bf16[256,5120]{1,0:T(8,128)(2,1)S(1)} fusion(f32[256,5120]{1,0:T(8,128)} %copy.22, f32[4,5120]{1,0:T(4,128)S(1)} %collective-permute-done.3, f32[4,5120]{1,0:T(4,128)S(1)} %collective-permute-done.2), kind=kLoop, calls=%fused_computation.10 | loop fusion | flops 5242880 | bytes 8028160 | tf_op jit(solution)/shard_map/convert_element_type | solution.py:65
  42.6 2.9 %collective-permute-start.4 = (bf16[256,5120]{1,0:T(8,128)(2,1)S(1)}, bf16[256,5120]{1,0:T(8,128)(2,1)S(1)}, u32[]{:S(2)}, u32[]{:S(2)}) collective-permute-start(bf16[256,5120]{1,0:T(8,128)(2,1)S(1)} %fusion.3), channel_id=1, source_target_pairs={{0,4},{4,8},{8,12},{12,16},{16,20},{20,24},{24,28},{1,5},{5,9},{9,... | collective-permute-start | bytes 7864328 | tf_op jit(solution)/shard_map/ppermute | solution.py:32
  45.6 3.7 %collective-permute-start.5 = (bf16[128,5120]{1,0:T(8,128)(2,1)S(1)}, bf16[128,5120]{1,0:T(8,128)(2,1)S(1)}, u32[]{:S(2)}, u32[]{:S(2)}) collective-permute-start(bf16[128,5120]{1,0:T(8,128)(2,1)S(1)} %slice.168), channel_id=1, source_target_pairs={{4,0},{8,4},{12,8},{16,12},{20,16},{24,20},{28,24},{5,1},{9,5},{13... | collective-permute-start | bytes 3932168 | tf_op jit(solution)/shard_map/ppermute | solution.py:32
  49.3 41.2 %collective-permute-done.4 = bf16[256,5120]{1,0:T(8,128)(2,1)S(1)} collective-permute-done((bf16[256,5120]{1,0:T(8,128)(2,1)S(1)}, bf16[256,5120]{1,0:T(8,128)(2,1)S(1)}, u32[]{:S(2)}, u32[]{:S(2)}) %collective-permute-start.4) | collective-permute-done | bytes 2621472 | tf_op jit(solution)/shard_map/ppermute | solution.py:32
  90.5 2.9 %fusion.19 = f32[1,512,512]{2,1,0:T(8,128)S(1)} fusion(bf16[256,5120]{1,0:T(8,128)(2,1)S(1)} %fusion.3, bf16[256,5120]{1,0:T(8,128)(2,1)S(1)} %collective-permute-done.4), kind=kOutput, calls=%fused_computation.31 | convolution fusion | flops 2694840320 | bytes 6291456 | tf_op jit(solution)/shard_map/dot_general | solution.py:74
  93.4 2.9 %fusion.18 = f32[1,512,512]{2,1,0:T(8,128)S(1)} fusion(bf16[128,5120]{1,0:T(8,128)(2,1)S(1)} %collective-permute-done.5, bf16[256,5120]{1,0:T(8,128)(2,1)S(1)} %fusion.3, bf16[256,5120]{1,0:T(8,128)(2,1)S(1)} %collective-permute-done.4), kind=kOutput, calls=%fused_computation.30 | convolution fusion | flops 2700083200 | bytes 7602176 | tf_op jit(solution)/shard_map/dot_general | solution.py:74
  96.3 1.5 pad_maximum_fusion.8
  97.9 87.9 %all-reduce.3.cloned.1.call-done = f32[2,512,512]{2,1,0:T(8,128)} async-done(((f32[2,512,512]{2,1,0:T(8,128)}), f32[2,512,512]{2,1,0:T(8,128)}) %all-reduce.3.cloned.1.call-update) | async-done | bytes 2097168 | tf_op jit(solution)/shard_map/psum | solution.py:82
  185.9 3.6 %fusion.16 = f32[2,512,16]{1,2,0:T(8,128)S(1)} fusion(f32[2,512,512]{2,1,0:T(8,128)} %all-reduce.3.cloned.1.call-done, f32[512,16]{0,1:T(8,128)S(1)} %copy-done), kind=kOutput, calls=%fused_computation.28 | convolution fusion | flops 101187584 | bytes 2195456 | tf_op jit(solution)/shard_map/wcd,wdr->wcr/dot_general | solution.py:85
  189.5 0.2 fusion.58
  189.8 3.1 %custom-call.16 = f32[2,16,16]{2,1,0:T(8,128)S(1)} custom-call(f32[2,16,16]{2,1,0:T(8,128)S(1)} %fusion.43), custom_call_target="Cholesky" | custom-call | tf_op jit(solution)/shard_map/jit(cholesky)/cholesky | solution.py:44
  193.1 2.5 custom-call.17
  195.6 0.3 convolution_bitcast_fusion.6
  195.9 3.5 %fusion.14 = f32[2,512,16]{1,2,0:T(8,128)S(1)} fusion(f32[2,512,16]{1,2,0:T(8,128)S(1)} %convolution_bitcast_fusion.6, f32[2,512,512]{2,1,0:T(8,128)} %all-reduce.3.cloned.1.call-done), kind=kOutput, calls=%fused_computation.26 | convolution fusion | flops 101187584 | bytes 2228224 | tf_op jit(solution)/shard_map/wcd,wdr->wcr/dot_general | solution.py:85
  199.4 0.2 fusion.59
  199.7 2.9 %custom-call.18 = f32[2,16,16]{2,1,0:T(8,128)S(1)} custom-call(f32[2,16,16]{2,1,0:T(8,128)S(1)} %fusion.41), custom_call_target="Cholesky" | custom-call | tf_op jit(solution)/shard_map/jit(cholesky)/cholesky | solution.py:44
  202.8 2.5 custom-call.19
  205.3 0.3 convolution_bitcast_fusion.5
  205.6 1.9 fusion.12
  207.5 0.2 fusion.60
  207.8 2.9 %custom-call.20 = f32[2,16,16]{2,1,0:T(8,128)S(1)} custom-call(f32[2,16,16]{2,1,0:T(8,128)S(1)} %fusion.39), custom_call_target="Cholesky" | custom-call | tf_op jit(solution)/shard_map/jit(cholesky)/cholesky | solution.py:44
  211.0 2.5 custom-call.21
  213.4 0.3 convolution_bitcast_fusion.4
  213.7 1.9 fusion.10
  215.7 0.2 fusion.61
  215.9 2.9 %custom-call.22 = f32[2,16,16]{2,1,0:T(8,128)S(1)} custom-call(f32[2,16,16]{2,1,0:T(8,128)S(1)} %fusion.37), custom_call_target="Cholesky" | custom-call | tf_op jit(solution)/shard_map/jit(cholesky)/cholesky | solution.py:44
  219.1 2.5 custom-call.23
  221.6 0.3 convolution_bitcast_fusion.3
  221.9 1.9 fusion.8
  223.8 0.2 fusion.62
  224.1 2.9 %custom-call.24 = f32[2,16,16]{2,1,0:T(8,128)S(1)} custom-call(f32[2,16,16]{2,1,0:T(8,128)S(1)} %fusion.35), custom_call_target="Cholesky" | custom-call | tf_op jit(solution)/shard_map/jit(cholesky)/cholesky | solution.py:44
  227.3 2.5 custom-call.25
  229.7 0.3 convolution_bitcast_fusion.2
  230.0 1.9 fusion.6
  231.9 0.2 fusion.63
  232.2 2.9 %custom-call.26 = f32[2,16,16]{2,1,0:T(8,128)S(1)} custom-call(f32[2,16,16]{2,1,0:T(8,128)S(1)} %fusion.33), custom_call_target="Cholesky" | custom-call | tf_op jit(solution)/shard_map/jit(cholesky)/cholesky | solution.py:44
  235.4 2.6 %custom-call.27 = f32[2,1,16,16]{2,3,1,0:T(8,128)S(1)} custom-call(f32[2,1,16,16]{3,2,1,0:T(8,128)S(1)} %select_bitcast_fusion), custom_call_target="InvertDiagBlocksLowerTriangular" | custom-call | tf_op jit(solution)/shard_map/triangular_solve/custom-call.0 | solution.py:45
  238.0 0.3 fusion.20
  238.3 5.3 %fusion = bf16[128,5120]{1,0:T(8,128)(2,1)} fusion(bf16[256,5120]{1,0:T(8,128)(2,1)} %copy-done.4, bf16[256,5120]{1,0:T(8,128)(2,1)} %copy-done.6, bf16[2,512,16]{1,2,0:T(8,128)(2,1)S(1)} %fusion.20), kind=kOutput, calls=%fused_computation.2 | convolution fusion | flops 117391360 | bytes 7884800 | tf_op jit(solution)/shard_map/dot_general | solution.py:94
  243.6 4.0 %fusion.1 = bf16[128,5120]{1,0:T(8,128)(2,1)} fusion(bf16[256,5120]{1,0:T(8,128)(2,1)S(1)} %copy-done.5, bf16[128,5120]{1,0:T(8,128)(2,1)} %copy-done.7, bf16[256,5120]{1,0:T(8,128)(2,1)} %copy-done.6, bf16[2,512,16]{1,2,0:T(8,128)(2,1)S(1)} %fusion.20), kind=kOutput, calls=%fused_computation.3 | convolution fusion | flops 122634240 | bytes 9195520 | tf_op jit(solution)/shard_map/dot_general | solution.py:94
  247.5 3.4 %pad_maximum_fusion.7 = bf16[256,5120]{1,0:T(8,128)(2,1)} fusion(bf16[128,5120]{1,0:T(8,128)(2,1)} %fusion.1, bf16[128,5120]{1,0:T(8,128)(2,1)} %fusion), kind=kLoop, calls=%fused_computation.14 | loop fusion | flops 5242880 | bytes 5242880 | tf_op jit(solution)/shard_map/concatenate | solution.py:100
  (67 shorter events, 3.2 us)
Async XLA Ops:
  6.5 179.3 %copy-start = (f32[512,16]{0,1:T(8,128)S(1)}, f32[512,16]{0,1:T(8,128)}, u32[]{:S(2)}) copy-start(f32[512,16]{0,1:T(8,128)} %param.8) | copy-start | bytes 98308
  6.5 8.4 %copy-start.2 = (bf16[256,5120]{1,0:T(8,128)(2,1)S(1)}, bf16[256,5120]{1,0:T(8,128)(2,1)}, u32[]{:S(2)}) copy-start(bf16[256,5120]{1,0:T(8,128)(2,1)} %param.6) | copy-start | bytes 7864324
  6.5 179.3 %all-reduce.3.cloned.1.call-start = ((), (), s32[]{:S(2)}) async-start(), calls=%async_computation | async-start | bytes 4194304 | tf_op jit(solution)/shard_map/psum | solution.py:82
  7.7 6.2 %collective-permute-start = (bf16[256,64]{1,0:T(8,128)(2,1)S(1)}, bf16[256,64]{1,0:T(8,128)(2,1)S(1)}, u32[]{:S(2)}, u32[]{:S(2)}) collective-permute-start(bf16[256,64]{1,0:T(8,128)(2,1)S(1)} %get-tuple-element.10), channel_id=1, source_target_pairs={{0,1},{1,2},{2,3},{4,5},{5,6},{6,7},{8,9},{9,10},{10,11},{12,13},{... | collective-permute-start | bytes 98312 | tf_op jit(solution)/shard_map/ppermute | solution.py:21
  11.1 6.3 %collective-permute-start.1 = (bf16[256,64]{1,0:T(8,128)(2,1)S(1)}, bf16[256,64]{1,0:T(8,128)(2,1)S(1)}, u32[]{:S(2)}, u32[]{:S(2)}) collective-permute-start(bf16[256,64]{1,0:T(8,128)(2,1)S(1)} %get-tuple-element.9), channel_id=1, source_target_pairs={{1,0},{2,1},{3,2},{5,4},{6,5},{7,6},{9,8},{10,9},{11,10},{13,12},{... | collective-permute-start | bytes 98312 | tf_op jit(solution)/shard_map/ppermute | solution.py:24
  19.1 2.3 copy-start.3
  21.5 16.3 %collective-permute-start.2 = (f32[4,5120]{1,0:T(4,128)S(1)}, f32[4,5120]{1,0:T(4,128)S(1)}, u32[]{:S(2)}, u32[]{:S(2)}) collective-permute-start(f32[4,5120]{1,0:T(4,128)S(1)} %bitcast.162), channel_id=1, source_target_pairs={{4,0},{8,4},{12,8},{16,12},{20,16},{24,20},{28,24},{5,1},{9,5},{13... | collective-permute-start | bytes 245768 | tf_op jit(solution)/shard_map/ppermute | solution.py:24
  24.0 13.8 %collective-permute-start.3 = (f32[4,5120]{1,0:T(4,128)S(1)}, f32[4,5120]{1,0:T(4,128)S(1)}, u32[]{:S(2)}, u32[]{:S(2)}) collective-permute-start(f32[4,5120]{1,0:T(4,128)S(1)} %bitcast.161), channel_id=1, source_target_pairs={{0,4},{4,8},{8,12},{12,16},{16,20},{20,24},{24,28},{1,5},{5,9},{9,... | collective-permute-start | bytes 245768 | tf_op jit(solution)/shard_map/ppermute | solution.py:21
  42.6 50.8 %copy-start.4 = (bf16[256,5120]{1,0:T(8,128)(2,1)}, bf16[256,5120]{1,0:T(8,128)(2,1)S(1)}, u32[]{:S(2)}) copy-start(bf16[256,5120]{1,0:T(8,128)(2,1)S(1)} %fusion.3) | copy-start | bytes 7864324
  42.6 47.9 %collective-permute-start.4 = (bf16[256,5120]{1,0:T(8,128)(2,1)S(1)}, bf16[256,5120]{1,0:T(8,128)(2,1)S(1)}, u32[]{:S(2)}, u32[]{:S(2)}) collective-permute-start(bf16[256,5120]{1,0:T(8,128)(2,1)S(1)} %fusion.3), channel_id=1, source_target_pairs={{0,4},{4,8},{8,12},{12,16},{16,20},{20,24},{24,28},{1,5},{5,9},{9,... | collective-permute-start | bytes 7864328 | tf_op jit(solution)/shard_map/ppermute | solution.py:32
  45.6 47.8 %collective-permute-start.5 = (bf16[128,5120]{1,0:T(8,128)(2,1)S(1)}, bf16[128,5120]{1,0:T(8,128)(2,1)S(1)}, u32[]{:S(2)}, u32[]{:S(2)}) collective-permute-start(bf16[128,5120]{1,0:T(8,128)(2,1)S(1)} %slice.168), channel_id=1, source_target_pairs={{4,0},{8,4},{12,8},{16,12},{20,16},{24,20},{28,24},{5,1},{9,5},{13... | collective-permute-start | bytes 3932168 | tf_op jit(solution)/shard_map/ppermute | solution.py:32
  90.5 2.9 %copy-start.6 = (bf16[256,5120]{1,0:T(8,128)(2,1)}, bf16[256,5120]{1,0:T(8,128)(2,1)S(1)}, u32[]{:S(2)}) copy-start(bf16[256,5120]{1,0:T(8,128)(2,1)S(1)} %collective-permute-done.4) | copy-start | bytes 7864324
  93.4 2.9 %copy-start.7 = (bf16[128,5120]{1,0:T(8,128)(2,1)}, bf16[128,5120]{1,0:T(8,128)(2,1)S(1)}, u32[]{:S(2)}) copy-start(bf16[128,5120]{1,0:T(8,128)(2,1)S(1)} %collective-permute-done.5) | copy-start | bytes 3932164
  185.9 19.7 %copy-start.1 = (f32[2,512,512]{2,1,0:T(8,128)S(1)}, f32[2,512,512]{2,1,0:T(8,128)}, u32[]{:S(2)}) copy-start(f32[2,512,512]{2,1,0:T(8,128)} %all-reduce.3.cloned.1.call-done) | copy-start | bytes 6291460
  238.3 5.3 %copy-start.5 = (bf16[256,5120]{1,0:T(8,128)(2,1)S(1)}, bf16[256,5120]{1,0:T(8,128)(2,1)}, u32[]{:S(2)}) copy-start(bf16[256,5120]{1,0:T(8,128)(2,1)} %copy-done.4) | copy-start | bytes 7864324
Sparse Core Ops, SparseCore 0:
  98.0 87.7 all-reduce.2
where the time goes:
time: 260 us; the launch traced here: 258 us
  waiting for transfers between devices  129 us (50%)
  other arithmetic  45 us (17%)
  matrix products  34.3 us (13%)
  local copies, waits for them, and re-layouts  19.7 us (8%)
  starting transfers between devices  15.8 us (6%)
  between operations  13.8 us (5%)
    psum x1, waiting for transfers between devices, per_device(): scatter_mat = lax.psum(partial_mats, 'ta') / total_time  87.9 us
    ppermute x2, waiting for transfers between devices, shifted(): lax.ppermute(value, axis, [(source, source + steps) for source in range(f...  41.2 us
    another operation x19, other arithmetic, orthonormal(): lower = jnp.linalg.cholesky(gram)  18.7 us
    another operation x13, other arithmetic, orthonormal(): lax.linalg.triangular_solve(lower, image, left_side=False, lower=True, tr...  15.4 us
    dot_general x6, matrix products, per_device(): jnp.einsum('wcd,wdr->wcr', scatter_mat, basis, precision=lax.Precision.HI...  14.8 us
    dot_general x2, matrix products, per_device(): jnp.dot(rounded[number, 2 * STRIDE:3 * STRIDE], coeffs, preferred_element...  9.23 us
    ppermute x2, starting transfers between devices, shifted(): lax.ppermute(value, axis, [(source, source + steps) for source in range(f...  6.64 us
    reshape x1, local copies, waits for them, and re-layouts, per_device(): filtered = jnp.einsum('bct,tu->cbu', pieces, band_matrix, preferred_eleme...  5.95 us
  transfers between devices with their start and end apart: 7, of which 2 were waited for; matrix products, arithmetic and copies ran while one was open for 8% of the time, Pallas kernels for 0%

commit v1 on v0

v1 whole, which is shorter than its diff:
```python
import functools

import jax
import jax.numpy as jnp
from jax import lax
from jax.experimental import pallas as pl
from jax.experimental.pallas import tpu as pltpu
from jax.sharding import PartitionSpec as P

TAPS = 129
GAUGE = 4
STRIDE = 128
RANK = 16
ITERS = 6
WIN = 512
BLOCK = 256
EDGE = 128
MESH = pl.DeviceIdType.MESH

PLACE = {2: 0, 3: 128, 1: 256, 0: 384, 4: 512}


def toeplitz_band(taps, width):
    count = taps.shape[0]
    line = jnp.concatenate([taps, jnp.zeros((width,), taps.dtype)])
    flat = jnp.tile(line, width)[: width * (count + width - 1)]
    return flat.reshape(width, count + width - 1).T


def dot_nt(a, b):
    return lax.dot_general(a, b, (((1,), (1,)), ((), ())), preferred_element_type=jnp.float32)


def inverse_factor(gram):
    columns = [jnp.broadcast_to(gram[:, j : j + 1], (RANK, 128)) for j in range(RANK)]
    row = lax.broadcasted_iota(jnp.int32, (RANK, 128), 0)
    lane = lax.broadcasted_iota(jnp.int32, (RANK, 128), 1)
    inverse = jnp.where(row == lane, 1.0, 0.0).astype(jnp.float32)
    diagonal = jnp.ones((RANK, 128), jnp.float32)
    for k in range(RANK):
        column = columns[k]
        pivot = column[k : k + 1, :]
        diagonal = jnp.where(row == k, pivot, diagonal)
        if k == RANK - 1:
            break
        scaled = jnp.where(row > k, column * (1.0 / pivot), 0.0)
        for j in range(k + 1, RANK):
            columns[j] = columns[j] - scaled * column[j : j + 1, :]
        inverse = inverse - scaled * inverse[k : k + 1, :]
    inverse = inverse * lax.rsqrt(diagonal)
    return inverse[:, :RANK]


def split(value):
    high = value.astype(jnp.bfloat16)
    return high, (value - high.astype(jnp.float32)).astype(jnp.bfloat16)


def kernel(
    nch, nta, raw, band, start, out,
    x, gz, part, recv, s_hi, s_lo, basis,
    own_sem, halo_send, halo_recv, part_send, part_recv, basis_send, basis_recv,
):
    c = lax.axis_index("ch")
    t = lax.axis_index("ta")
    chans, samples = raw.shape
    right = EDGE + samples
    owners = (nta // 2 - 1, nta // 2)

    def exists(dc, dt):
        return (c + dc >= 0) & (c + dc < nch) & (t + dt >= 0) & (t + dt < nta)

    partners = [(dc, dt) for dc in (-2, -1, 0, 1, 2) for dt in (-1, 0, 1) if (dc, dt) != (0, 0)]
    partners += [(0, dt) for dt in range(1 - nta, nta) if abs(dt) > 1]

    own = pltpu.make_async_copy(raw, x.at[272:528, EDGE:right], own_sem)
    own.start()

    barrier = pltpu.get_barrier_semaphore()
    for dc, dt in partners:
        @pl.when(exists(dc, dt))
        def _():
            pl.semaphore_signal(barrier, inc=1, device_id=(c + dc, t + dt), device_id_type=MESH)
    near = 1 + sum(((c + dc >= 0) & (c + dc < nch)).astype(jnp.int32) for dc in (-2, -1, 1, 2))
    around = 1 + sum(((t + dt >= 0) & (t + dt < nta)).astype(jnp.int32) for dt in (-1, 1))
    pl.semaphore_wait(barrier, near * around - 1 + nta - around)

    mid = (EDGE, right)
    whole = (0, samples)
    low, high = (0, EDGE), (right, right + EDGE)
    head, tail = (0, EDGE), (samples - EDGE, samples)
    kinds = [
        (0, 1, (0, 256), tail, (272, 528), low),
        (0, -1, (0, 256), head, (272, 528), high),
        (1, 0, (240, 256), whole, (256, 272), mid),
        (-1, 0, (0, 16), whole, (528, 544), mid),
        (1, 1, (0, 256), tail, (16, 272), low),
        (1, -1, (0, 256), head, (16, 272), high),
        (-1, 1, (0, 144), tail, (528, 672), low),
        (-1, -1, (0, 144), head, (528, 672), high),
        (2, 0, (240, 256), whole, (0, 16), mid),
        (2, 1, (240, 256), tail, (0, 16), low),
        (2, -1, (240, 256), head, (0, 16), high),
        (1, 0, (112, 240), whole, (128, 256), mid),
        (-1, 0, (16, 144), whole, (544, 672), mid),
        (1, 0, (0, 112), whole, (16, 128), mid),
    ]

    def halo(index):
        dc, dt, rows, cols, to_rows, to_cols = kinds[index]
        return pltpu.make_async_remote_copy(
            src_ref=raw.at[rows[0] : rows[1], cols[0] : cols[1]],
            dst_ref=x.at[to_rows[0] : to_rows[1], to_cols[0] : to_cols[1]],
            send_sem=halo_send.at[index],
            recv_sem=halo_recv.at[index],
            device_id=(c + dc, t + dt),
            device_id_type=MESH,
        )

    def each_halo(indices, sign, act):
        for index in indices:
            dc, dt = kinds[index][:2]
            @pl.when(exists(sign * dc, sign * dt))
            def _():
                act(halo(index))

    everything = range(len(kinds))
    each_halo(everything, 1, lambda copy: copy.start())

    @pl.when(t == 0)
    def _():
        x[:, 0:EDGE] = jnp.zeros((x.shape[0], EDGE), x.dtype)

    @pl.when(t == nta - 1)
    def _():
        x[:, right : right + EDGE] = jnp.zeros((x.shape[0], EDGE), x.dtype)

    @pl.when(c == 0)
    def _():
        x[256:272, :] = jnp.zeros((16, x.shape[1]), x.dtype)

    @pl.when(c == 1)
    def _():
        x[0:16, :] = jnp.zeros((16, x.shape[1]), x.dtype)

    @pl.when(c == nch - 1)
    def _():
        x[528:544, :] = jnp.zeros((16, x.shape[1]), x.dtype)
        gz[512:640, :] = jnp.zeros((STRIDE, samples), gz.dtype)

    @pl.when(c == 0)
    def _():
        gz[256:512, :] = jnp.zeros((2 * STRIDE, samples), gz.dtype)

    def gauge(first, count):
        rows = STRIDE * count + 32
        @pl.loop(0, samples // BLOCK)
        def _(number):
            start_col = pl.multiple_of(number * BLOCK, BLOCK)
            piece = x[STRIDE * first : STRIDE * first + rows, pl.ds(start_col, 2 * BLOCK)]
            filtered = jnp.dot(piece, band[...], preferred_element_type=jnp.float32)
            for step in range(count):
                base = STRIDE * step
                upper = filtered[base + 20 : base + 20 + STRIDE]
                lower = filtered[base + 12 : base + 12 + STRIDE]
                place = PLACE[first + step]
                gz[place : place + STRIDE, pl.ds(start_col, BLOCK)] = (upper - lower).astype(gz.dtype)

    def products(groups):
        chunk = 1024
        for left, right_tile, place in groups:
            part[place : place + left[1] - left[0], :] = jnp.zeros((left[1] - left[0], STRIDE), jnp.float32)
        @pl.loop(0, samples // chunk)
        def _(number):
            cols = pl.ds(pl.multiple_of(number * chunk, chunk), chunk)
            for left, right_tile, place in groups:
                part[place : place + left[1] - left[0], :] += dot_nt(
                    gz[left[0] : left[1], cols], gz[right_tile : right_tile + STRIDE, cols]
                )

    spans = {
        ("own", 0): (0, 384, 0), ("own", 1): (0, 384, 0),
        ("next", 0): (384, 768, 384), ("next", 1): (384, 768, 384),
        ("far", 0): (1280, 1792, 768), ("far", 1): (768, 1280, 768),
    }
    order = {"own": 0, "next": 1, "far": 2}

    def part_copy(stage, window, source):
        begin, end, land = spans[stage, window]
        return pltpu.make_async_remote_copy(
            src_ref=part.at[begin:end],
            dst_ref=recv.at[source, land : land + end - begin],
            send_sem=part_send.at[window, order[stage]],
            recv_sem=part_recv.at[source, order[stage]],
            device_id=(c, owners[window]),
            device_id_type=MESH,
        )

    def send_part(stage, window):
        @pl.when(t != owners[window])
        def _():
            part_copy(stage, window, t).start()

    own.wait()
    each_halo(range(0, 8), -1, lambda copy: copy.wait_recv())
    gauge(2, 2)
    products([((0, 256), 0, 0), ((128, 256), 128, 256)])
    send_part("own", 0)
    send_part("own", 1)

    each_halo([11], -1, lambda copy: copy.wait_recv())
    @pl.when(c > 0)
    def _():
        gauge(1, 1)
    products([((0, 384), 256, 384)])
    send_part("next", 0)
    send_part("next", 1)

    each_halo([12], -1, lambda copy: copy.wait_recv())
    @pl.when(c < nch - 1)
    def _():
        gauge(4, 1)
    products([((0, 384), 512, 768), ((512, 640), 512, 1152)])
    send_part("far", 1)

    each_halo([8, 9, 10, 13], -1, lambda copy: copy.wait_recv())
    @pl.when(c > 0)
    def _():
        gauge(0, 1)
    products([((0, 512), 384, 1280)])
    send_part("far", 0)

    total_time = samples * nta

    def solve(window):
        for source in range(nta):
            if source != owners[window]:
                for stage in order:
                    part_copy(stage, window, source).wait_recv()

        blocks = {
            (0, 0): ("own", 0), (1, 0): ("own", 1), (1, 1): ("own", 2),
            (0, 2): ("next", 0), (1, 2): ("next", 1), (2, 2): ("next", 2),
            (0, 3): ("far", 0), (1, 3): ("far", 1), (2, 3): ("far", 2), (3, 3): ("far", 3),
        }
        for (p, q), (stage, number) in blocks.items():
            begin, _, land = spans[stage, window]
            begin, land = begin + STRIDE * number, land + STRIDE * number
            value = part[begin : begin + STRIDE, :]
            for source in range(nta):
                if source != owners[window]:
                    value = value + recv[source, land : land + STRIDE, :]
            value = value * (1.0 / total_time)
            for row, col, block in ((p, q, value), (q, p, value.T)):
                if (row, col) == (p, q) or p != q:
                    high_part, low_part = split(block)
                    where = (slice(STRIDE * row, STRIDE * (row + 1)), slice(STRIDE * col, STRIDE * (col + 1)))
                    s_hi[where] = high_part
                    s_lo[where] = low_part

        def sweep(_, current):
            high_part, low_part = split(current)
            both = jnp.concatenate([high_part, low_part], axis=0)
            image = jnp.dot(both, s_hi[...], preferred_element_type=jnp.float32)
            image = image[:RANK] + image[RANK:] + jnp.dot(
                high_part, s_lo[...], preferred_element_type=jnp.float32
            )
            gram = lax.dot_general(
                image, image, (((1,), (1,)), ((), ())),
                precision=lax.Precision.HIGHEST, preferred_element_type=jnp.float32,
            )
            return jnp.dot(
                inverse_factor(gram), image,
                precision=lax.Precision.HIGHEST, preferred_element_type=jnp.float32,
            )

        found = lax.fori_loop(0, ITERS, sweep, start[window]).astype(jnp.bfloat16)
        zero = jnp.zeros((RANK, STRIDE), jnp.bfloat16)
        last = [found[:, 384:512], zero] if window == 0 else [zero, found[:, 384:512]]
        basis[window] = jnp.concatenate([found[:, :384]] + last, axis=1)

    def basis_copy(window, target):
        return pltpu.make_async_remote_copy(
            src_ref=basis.at[window],
            dst_ref=basis.at[window],
            send_sem=basis_send.at[window, target],
            recv_sem=basis_recv.at[window],
            device_id=(c, target),
            device_id_type=MESH,
        )

    for window in (0, 1):
        @pl.when(t == owners[window])
        def _():
            solve(window)
            for target in range(nta):
                if target != owners[window]:
                    basis_copy(window, target).start()

    for window in (0, 1):
        @pl.when(t != owners[window])
        def _():
            basis_copy(window, owners[window]).wait_recv()

    both = jnp.concatenate([basis[0], basis[1]], axis=0)
    nothing = jnp.zeros((RANK, STRIDE), jnp.bfloat16)
    kept = jnp.concatenate(
        [
            jnp.concatenate([basis[0][:, 0:128], nothing], axis=1),
            jnp.concatenate([nothing, basis[1][:, 128:256]], axis=1),
        ],
        axis=0,
    )

    @pl.loop(0, samples // 512)
    def _(number):
        cols = pl.ds(pl.multiple_of(number * 512, 512), 512)
        coeffs = jnp.dot(both, gz[:, cols], preferred_element_type=jnp.float32).astype(jnp.bfloat16)
        fitted = lax.dot_general(
            kept, coeffs, (((0,), (0,)), ((), ())), preferred_element_type=jnp.float32
        )
        out[:, cols] = (gz[0:256, cols].astype(jnp.float32) - fitted).astype(out.dtype)

    each_halo(everything, 1, lambda copy: copy.wait_send())
    for window in (0, 1):
        @pl.when(t != owners[window])
        def _():
            for stage in order:
                part_copy(stage, window, t).wait_send()
        @pl.when(t == owners[window])
        def _():
            for target in range(nta):
                if target != owners[window]:
                    basis_copy(window, target).wait_send()


def per_device(nch, nta, raw, fir_taps, start_basis):
    chans, samples = raw.shape
    band = jnp.pad(toeplitz_band(fir_taps, BLOCK), ((64, 64), (0, 0)))
    tiles = start_basis.T.reshape(RANK, 4, STRIDE)
    start = jnp.stack([tiles[:, jnp.array(o), :].reshape(RANK, WIN) for o in ([2, 3, 1, 0], [1, 2, 0, 3])])
    vmem = pl.BlockSpec(memory_space=pltpu.VMEM)
    return pl.pallas_call(
        functools.partial(kernel, nch, nta),
        out_shape=jax.ShapeDtypeStruct((chans, samples), jnp.bfloat16),
        in_specs=[pl.BlockSpec(memory_space=pl.ANY), vmem, vmem],
        out_specs=vmem,
        scratch_shapes=[
            pltpu.VMEM((672, samples + 2 * EDGE), jnp.bfloat16),
            pltpu.VMEM((640, samples), jnp.bfloat16),
            pltpu.VMEM((14 * STRIDE, STRIDE), jnp.float32),
            pltpu.VMEM((nta, 10 * STRIDE, STRIDE), jnp.float32),
            pltpu.VMEM((WIN, WIN), jnp.bfloat16),
            pltpu.VMEM((WIN, WIN), jnp.bfloat16),
            pltpu.VMEM((2, RANK, 640), jnp.bfloat16),
            pltpu.SemaphoreType.DMA,
            pltpu.SemaphoreType.DMA((14,)),
            pltpu.SemaphoreType.DMA((14,)),
            pltpu.SemaphoreType.DMA((2, 3)),
            pltpu.SemaphoreType.DMA((nta, 3)),
            pltpu.SemaphoreType.DMA((2, nta)),
            pltpu.SemaphoreType.DMA((2,)),
        ],
        compiler_params=pltpu.CompilerParams(
            collective_id=0, has_side_effects=True, vmem_limit_bytes=48 * 1024 * 1024
        ),
    )(raw, band, start)


def solution(mesh):
    sizes = dict(mesh.shape)
    return jax.shard_map(
        functools.partial(per_device, sizes["ch"], sizes["ta"]),
        mesh=mesh,
        in_specs=(P("ch", "ta"), P(), P()),
        out_specs=P("ch", "ta"),
        check_vma=False,
    )
```

time: 260 us -> 88.9 us (0.34)
  waiting for transfers between devices: 129 us -> 0 us
  Pallas kernels: 0 us -> 83 us
  other arithmetic: 45 us -> 1.33 us
  matrix products: 34.3 us -> 0 us
  starting transfers between devices: 15.8 us -> 0 us
  local copies, waits for them, and re-layouts: 19.7 us -> 4.37 us
  between operations: 13.8 us -> 0.11 us
    psum x1 -> x0, waiting for transfers between devices: 87.9 us -> none  [per_device(): scatter_mat = lax.psum(partial_mats, 'ta') / total_time]
    pallas_call x0 -> x1, Pallas kernels: none -> 83 us  [per_device(): pl.pallas_call(functools.partial(kernel, nch, nta), out_shape=jax.ShapeDt...]
    ppermute x6 -> x0, waiting for transfers between devices: 41.2 us -> none  [the longest x2 41.2 us: shifted(): lax.ppermute(value, axis, [(source, source + steps) for source in range(f...]
    another operation x34 -> x1, other arithmetic: 35.8 us -> 0.01 us  [per_device(): jnp.stack([tiles[:, jnp.array(o), :].reshape(RANK, WIN) for o in ([2, 3,...]
    dot_general x17 -> x0, matrix products: 32.6 us -> none  [the longest x6 14.8 us: per_device(): jnp.einsum('wcd,wdr->wcr', scatter_mat, basis, precision=lax.Precision.HI...]
    ppermute x6 -> x0, starting transfers between devices: 15.8 us -> none  [the longest x2 6.64 us: shifted(): lax.ppermute(value, axis, [(source, source + steps) for source in range(f...]
    reshape x1, local copies, waits for them, and re-layouts: 5.95 us -> 0.01 us  [per_device(): tiles = start_basis.T.reshape(RANK, 4, STRIDE)]
    transpose x1 -> x0, local copies, waits for them, and re-layouts: 5.93 us -> none  [per_device(): jnp.einsum('bct,tu->cbu', pieces, band_matrix, preferred_element_type=jnp...]
  transfers between devices with their start and end apart: 7 -> 0, of which waited for: 2 -> 0; matrix products, arithmetic and copies ran while one was open for 8% -> 0% of each run, Pallas kernels for 0% -> 0%
where the time goes in v1:
time: 88.9 us; the launch traced here: 88.8 us
  Pallas kernels  83 us (93%)
  local copies, waits for them, and re-layouts  4.37 us (5%)
  other arithmetic  1.33 us (1%)
    pallas_call x1, Pallas kernels, per_device(): pl.pallas_call(functools.partial(kernel, nch, nta), out_shape=jax.ShapeDt...  83 us

profile of v1, /device:TPU:4, one launch (start us, length us, event | category | flops | bytes accessed | tf_op | source)
XLA Modules:
  0.0 88.8 jit_solution(213042922285366723)
XLA Ops:
  0.0 0.0 copy-start
  0.0 0.0 copy-start.1
  0.0 0.8 concatenate.3
  0.8 0.7 pad_clamp_fusion.1
  1.5 0.7 pad_clamp_fusion
  2.1 0.0 copy-done
  2.1 0.6 gather_fusion.1
  2.7 0.6 gather_fusion
  3.4 0.6 tile.10
  4.0 0.1 reshape.7
  4.1 0.1 copy.9
  4.3 0.0 copy-done.1
  4.3 83.0 %shard_map.55 = bf16[256,5120]{1,0:T(8,128)(2,1)S(1)} custom-call(bf16[256,5120]{1,0:T(8,128)(2,1)S(1)} %copy-done.1, bf16[512,256]{1,0:T(8,128)(2,1)S(1)} %pad.5.band, f32[2,16,512]{2,1,0:T(8,128)S(1)} %pad_maximum_fusion.start), custom_call_target="tpu_custom_call" | custom-call | tf_op jit(solution)/shard_map/pallas_call | solution.py:343
  87.3 1.5 %copy.17 = bf16[256,5120]{1,0:T(8,128)(2,1)} copy(bf16[256,5120]{1,0:T(8,128)(2,1)S(1)} %shard_map.55) | data formatting | bytes 5242880
  (9 shorter events, 0.1 us)
Async XLA Ops:
  0.0 2.1 %copy-start = (f32[512,16]{0,1:T(8,128)S(1)}, f32[512,16]{0,1:T(8,128)}, u32[]{:S(2)}) copy-start(f32[512,16]{0,1:T(8,128)} %param.7) | copy-start | bytes 98308
  0.0 4.3 %copy-start.1 = (bf16[256,5120]{1,0:T(8,128)(2,1)S(1)}, bf16[256,5120]{1,0:T(8,128)(2,1)}, u32[]{:S(2)}) copy-start(bf16[256,5120]{1,0:T(8,128)(2,1)} %raw.1) | copy-start | bytes 7864324

commit v2 on v1

--- a/solution.py
+++ b/solution.py
@@ -20,13 +20,6 @@
 PLACE = {2: 0, 3: 128, 1: 256, 0: 384, 4: 512}
 
 
-def toeplitz_band(taps, width):
-    count = taps.shape[0]
-    line = jnp.concatenate([taps, jnp.zeros((width,), taps.dtype)])
-    flat = jnp.tile(line, width)[: width * (count + width - 1)]
-    return flat.reshape(width, count + width - 1).T
-
-
 def dot_nt(a, b):
     return lax.dot_general(a, b, (((1,), (1,)), ((), ())), preferred_element_type=jnp.float32)
 
@@ -35,7 +28,7 @@
     columns = [jnp.broadcast_to(gram[:, j : j + 1], (RANK, 128)) for j in range(RANK)]
     row = lax.broadcasted_iota(jnp.int32, (RANK, 128), 0)
     lane = lax.broadcasted_iota(jnp.int32, (RANK, 128), 1)
-    inverse = jnp.where(row == lane, 1.0, 0.0).astype(jnp.float32)
+    inverse = jnp.where(row == lane % RANK, 1.0, 0.0).astype(jnp.float32)
     diagonal = jnp.ones((RANK, 128), jnp.float32)
     for k in range(RANK):
         column = columns[k]
@@ -47,8 +40,7 @@
         for j in range(k + 1, RANK):
             columns[j] = columns[j] - scaled * column[j : j + 1, :]
         inverse = inverse - scaled * inverse[k : k + 1, :]
-    inverse = inverse * lax.rsqrt(diagonal)
-    return inverse[:, :RANK]
+    return inverse * lax.rsqrt(diagonal)
 
 
 def split(value):
@@ -56,9 +48,35 @@
     return high, (value - high.astype(jnp.float32)).astype(jnp.bfloat16)
 
 
+def split_three(value):
+    high = value.astype(jnp.bfloat16)
+    rest = value - high.astype(jnp.float32)
+    middle = rest.astype(jnp.bfloat16)
+    return high, middle, (rest - middle.astype(jnp.float32)).astype(jnp.bfloat16)
+
+
+def gram_of(parts):
+    stacked = jnp.concatenate(parts, axis=0)
+    terms = dot_nt(stacked, stacked)
+    rows = terms[:RANK] + (terms[RANK : 2 * RANK] + terms[2 * RANK :])
+    return rows[:, :RANK] + (rows[:, RANK : 2 * RANK] + rows[:, 2 * RANK :])
+
+
+def apply_inverse(inverse, parts):
+    lane = lax.broadcasted_iota(jnp.int32, inverse.shape, 1)
+    high, middle, low = (part.astype(jnp.float32) for part in split_three(inverse))
+    left = jnp.where(lane < 3 * RANK, high, jnp.where(lane < 5 * RANK, middle, low))
+    left = jnp.where(lane < 6 * RANK, left, 0.0).astype(jnp.bfloat16)
+    zero = jnp.zeros((2 * RANK, WIN), jnp.bfloat16)
+    right = jnp.concatenate(
+        [parts[0], parts[1], parts[2], parts[0], parts[1], parts[0], zero], axis=0
+    )
+    return jnp.dot(left, right, preferred_element_type=jnp.float32)
+
+
 def kernel(
-    nch, nta, raw, band, start, out,
-    x, gz, part, recv, s_hi, s_lo, basis,
+    nch, nta, raw, taps, start, out,
+    x, gz, band, part, recv, s_hi, s_lo, basis,
     own_sem, halo_send, halo_recv, part_send, part_recv, basis_send, basis_recv,
 ):
     c = lax.axis_index("ch")
@@ -127,6 +145,10 @@
     everything = range(len(kinds))
     each_halo(everything, 1, lambda copy: copy.start())
 
+    lines = jnp.broadcast_to(taps[...], (BLOCK, 2 * BLOCK))
+    lines = pltpu.roll(lines, 64, 1, stride=1, stride_axis=0)
+    band[...] = lines.T.astype(band.dtype)
+
     @pl.when(t == 0)
     def _():
         x[:, 0:EDGE] = jnp.zeros((x.shape[0], EDGE), x.dtype)
@@ -216,19 +238,29 @@
     send_part("next", 0)
     send_part("next", 1)
 
-    each_halo([12], -1, lambda copy: copy.wait_recv())
-    @pl.when(c < nch - 1)
-    def _():
-        gauge(4, 1)
-    products([((0, 384), 512, 768), ((512, 640), 512, 1152)])
-    send_part("far", 1)
-
-    each_halo([8, 9, 10, 13], -1, lambda copy: copy.wait_recv())
-    @pl.when(c > 0)
-    def _():
-        gauge(0, 1)
-    products([((0, 512), 384, 1280)])
-    send_part("far", 0)
+    def tile_after():
+        each_halo([12], -1, lambda copy: copy.wait_recv())
+        @pl.when(c < nch - 1)
+        def _():
+            gauge(4, 1)
+        products([((0, 384), 512, 768), ((512, 640), 512, 1152)])
+        send_part("far", 1)
+
+    def first_tile():
+        each_halo([8, 9, 10, 13], -1, lambda copy: copy.wait_recv())
+        @pl.when(c > 0)
+        def _():
+            gauge(0, 1)
+        products([((0, 512), 384, 1280)])
+        send_part("far", 0)
+
+    @pl.when(c % 2 == 1)
+    def _():
+        first_tile()
+    tile_after()
+    @pl.when(c % 2 == 0)
+    def _():
+        first_tile()
 
     total_time = samples * nta
 
@@ -265,16 +297,12 @@
             image = image[:RANK] + image[RANK:] + jnp.dot(
                 high_part, s_lo[...], preferred_element_type=jnp.float32
             )
-            gram = lax.dot_general(
-                image, image, (((1,), (1,)), ((), ())),
-                precision=lax.Precision.HIGHEST, preferred_element_type=jnp.float32,
-            )
-            return jnp.dot(
-                inverse_factor(gram), image,
-                precision=lax.Precision.HIGHEST, preferred_element_type=jnp.float32,
-            )
-
-        found = lax.fori_loop(0, ITERS, sweep, start[window]).astype(jnp.bfloat16)
+            parts = split_three(image)
+            return apply_inverse(inverse_factor(gram_of(parts)), parts)
+
+        places = (2, 3, 1, 0) if window == 0 else (1, 2, 0, 3)
+        first = jnp.concatenate([start[:, STRIDE * p : STRIDE * (p + 1)] for p in places], axis=1)
+        found = lax.fori_loop(0, ITERS, sweep, first).astype(jnp.bfloat16)
         zero = jnp.zeros((RANK, STRIDE), jnp.bfloat16)
         last = [found[:, 384:512], zero] if window == 0 else [zero, found[:, 384:512]]
         basis[window] = jnp.concatenate([found[:, :384]] + last, axis=1)
@@ -336,9 +364,7 @@
 
 def per_device(nch, nta, raw, fir_taps, start_basis):
     chans, samples = raw.shape
-    band = jnp.pad(toeplitz_band(fir_taps, BLOCK), ((64, 64), (0, 0)))
-    tiles = start_basis.T.reshape(RANK, 4, STRIDE)
-    start = jnp.stack([tiles[:, jnp.array(o), :].reshape(RANK, WIN) for o in ([2, 3, 1, 0], [1, 2, 0, 3])])
+    taps = jnp.pad(fir_taps.astype(jnp.float32), (0, 2 * BLOCK - TAPS))[None]
     vmem = pl.BlockSpec(memory_space=pltpu.VMEM)
     return pl.pallas_call(
         functools.partial(kernel, nch, nta),
@@ -348,6 +374,7 @@
         scratch_shapes=[
             pltpu.VMEM((672, samples + 2 * EDGE), jnp.bfloat16),
             pltpu.VMEM((640, samples), jnp.bfloat16),
+            pltpu.VMEM((2 * BLOCK, BLOCK), jnp.bfloat16),
             pltpu.VMEM((14 * STRIDE, STRIDE), jnp.float32),
             pltpu.VMEM((nta, 10 * STRIDE, STRIDE), jnp.float32),
             pltpu.VMEM((WIN, WIN), jnp.bfloat16),
@@ -364,7 +391,7 @@
         compiler_params=pltpu.CompilerParams(
             collective_id=0, has_side_effects=True, vmem_limit_bytes=48 * 1024 * 1024
         ),
-    )(raw, band, start)
+    )(raw, taps, start_basis.T)
 
 
 def solution(mesh):

time: 88.9 us -> 88 us (0.990)
    unnamed x5, local copies, waits for them, and re-layouts: 1.5 us -> 3.99 us
    gather x2 -> x0, other arithmetic: 1.32 us -> none  [per_device(): tiles[:, jnp.array(o), :].reshape(RANK, WIN)]
    gather x4 -> x0, local copies, waits for them, and re-layouts: 1.13 us -> none  [per_device(): tiles[:, jnp.array(o), :].reshape(RANK, WIN)]
where the time goes in v2:
time: 88 us; the launch traced here: 87.8 us
  Pallas kernels  83.1 us (94%)
  local copies, waits for them, and re-layouts  3.99 us (5%)
    pallas_call x1, Pallas kernels, per_device(): pl.pallas_call(functools.partial(kernel, nch, nta), out_shape=jax.ShapeDt...  83.1 us
    unnamed x5, local copies, waits for them, and re-layouts  3.99 us

profile of v2, /device:TPU:4, one launch (start us, length us, event | category | flops | bytes accessed | tf_op | source)
XLA Modules:
  0.0 87.8 jit_solution(1032365889819682811)
XLA Ops:
  0.0 0.7 pad_convert_fusion
  0.7 0.0 copy-start
  0.7 1.7 %copy-done = bf16[256,5120]{1,0:T(8,128)(2,1)S(1)} copy-done((bf16[256,5120]{1,0:T(8,128)(2,1)S(1)}, bf16[256,5120]{1,0:T(8,128)(2,1)}, u32[]{:S(2)}) %copy-start) | copy-done | bytes 2621464
  2.4 0.0 copy-start.1
  2.4 0.8 copy-done.1
  3.2 83.1 %shard_map.37 = bf16[256,5120]{1,0:T(8,128)(2,1)S(1)} custom-call(bf16[256,5120]{1,0:T(8,128)(2,1)S(1)} %copy-done, f32[1,512]{1,0:T(1,128)S(1)} %bitcast.3, f32[16,512]{1,0:T(8,128)S(1)} %bitcast.2), custom_call_target="tpu_custom_call" | custom-call | tf_op jit(solution)/shard_map/pallas_call | solution.py:369
  86.3 1.5 %copy.5 = bf16[256,5120]{1,0:T(8,128)(2,1)} copy(bf16[256,5120]{1,0:T(8,128)(2,1)S(1)} %shard_map.37) | data formatting | bytes 5242880
Async XLA Ops:
  0.7 1.7 %copy-start = (bf16[256,5120]{1,0:T(8,128)(2,1)S(1)}, bf16[256,5120]{1,0:T(8,128)(2,1)}, u32[]{:S(2)}) copy-start(bf16[256,5120]{1,0:T(8,128)(2,1)} %raw.1) | copy-start | bytes 7864324
  2.4 0.8 copy-start.1

commit v3 on v2

--- a/solution.py
+++ b/solution.py
@@ -1,4 +1,5 @@
 import functools
+import math
 
 import jax
 import jax.numpy as jnp
@@ -30,16 +31,31 @@
     lane = lax.broadcasted_iota(jnp.int32, (RANK, 128), 1)
     inverse = jnp.where(row == lane % RANK, 1.0, 0.0).astype(jnp.float32)
     diagonal = jnp.ones((RANK, 128), jnp.float32)
-    for k in range(RANK):
-        column = columns[k]
-        pivot = column[k : k + 1, :]
-        diagonal = jnp.where(row == k, pivot, diagonal)
-        if k == RANK - 1:
-            break
-        scaled = jnp.where(row > k, column * (1.0 / pivot), 0.0)
-        for j in range(k + 1, RANK):
-            columns[j] = columns[j] - scaled * column[j : j + 1, :]
-        inverse = inverse - scaled * inverse[k : k + 1, :]
+
+    def spread(value, index):
+        return jnp.broadcast_to(value[index : index + 1, :], (RANK, 128))
+
+    for first in range(0, RANK, 4):
+        block = range(first, first + 4)
+        lead = {(i, j): spread(columns[j], i) for j in block for i in block if i >= j}
+        lines = {k: spread(inverse, k) for k in block}
+        scaled = {}
+        for k in block:
+            pivot = lead[k, k]
+            diagonal = jnp.where(row == k, pivot, diagonal)
+            reciprocal = 1.0 / pivot
+            scaled[k] = jnp.where(row > k, columns[k] * reciprocal, 0.0)
+            for j in range(k + 1, first + 4):
+                ratio = lead[j, k] * reciprocal
+                for i in range(j, first + 4):
+                    lead[i, j] = lead[i, j] - ratio * lead[i, k]
+                columns[j] = columns[j] - scaled[k] * lead[j, k]
+                lines[j] = lines[j] - ratio * lines[k]
+        for j in range(first + 4, RANK):
+            for k in block:
+                columns[j] = columns[j] - scaled[k] * spread(columns[k], j)
+        for k in block:
+            inverse = inverse - scaled[k] * lines[k]
     return inverse * lax.rsqrt(diagonal)
 
 
@@ -75,8 +91,8 @@
 
 
 def kernel(
-    nch, nta, raw, taps, start, out,
-    x, gz, band, part, recv, s_hi, s_lo, basis,
+    nch, nta, raw, taps_in, start_in, out,
+    taps, start, small_sem, x, gz, band, part, recv, s_hi, s_lo, basis,
     own_sem, halo_send, halo_recv, part_send, part_recv, basis_send, basis_recv,
 ):
     c = lax.axis_index("ch")
@@ -93,6 +109,10 @@
 
     own = pltpu.make_async_copy(raw, x.at[272:528, EDGE:right], own_sem)
     own.start()
+    taps_copy = pltpu.make_async_copy(taps_in, taps, small_sem.at[0])
+    start_copy = pltpu.make_async_copy(start_in, start, small_sem.at[1])
+    taps_copy.start()
+    start_copy.start()
 
     barrier = pltpu.get_barrier_semaphore()
     for dc, dt in partners:
@@ -145,6 +165,8 @@
     everything = range(len(kinds))
     each_halo(everything, 1, lambda copy: copy.start())
 
+    taps_copy.wait()
+    start_copy.wait()
     lines = jnp.broadcast_to(taps[...], (BLOCK, 2 * BLOCK))
     lines = pltpu.roll(lines, 64, 1, stride=1, stride_axis=0)
     band[...] = lines.T.astype(band.dtype)
@@ -176,17 +198,26 @@
 
     def gauge(first, count):
         rows = STRIDE * count + 32
-        @pl.loop(0, samples // BLOCK)
+        together = math.gcd(samples // BLOCK, 5)
+        @pl.loop(0, samples // (BLOCK * together))
         def _(number):
-            start_col = pl.multiple_of(number * BLOCK, BLOCK)
-            piece = x[STRIDE * first : STRIDE * first + rows, pl.ds(start_col, 2 * BLOCK)]
-            filtered = jnp.dot(piece, band[...], preferred_element_type=jnp.float32)
-            for step in range(count):
-                base = STRIDE * step
-                upper = filtered[base + 20 : base + 20 + STRIDE]
-                lower = filtered[base + 12 : base + 12 + STRIDE]
-                place = PLACE[first + step]
-                gz[place : place + STRIDE, pl.ds(start_col, BLOCK)] = (upper - lower).astype(gz.dtype)
+            start_col = pl.multiple_of(number * (BLOCK * together), BLOCK)
+            pieces = [
+                x[STRIDE * first : STRIDE * first + rows, pl.ds(start_col + BLOCK * p, 2 * BLOCK)]
+                for p in range(together)
+            ]
+            filtered = jnp.dot(
+                jnp.concatenate(pieces, axis=0), band[...], preferred_element_type=jnp.float32
+            )
+            for p in range(together):
+                for step in range(count):
+                    base = rows * p + STRIDE * step
+                    upper = filtered[base + 20 : base + 20 + STRIDE]
+                    lower = filtered[base + 12 : base + 12 + STRIDE]
+                    place = PLACE[first + step]
+                    gz[place : place + STRIDE, pl.ds(start_col + BLOCK * p, BLOCK)] = (
+                        upper - lower
+                    ).astype(gz.dtype)
 
     def products(groups):
         chunk = 1024
@@ -369,9 +400,12 @@
     return pl.pallas_call(
         functools.partial(kernel, nch, nta),
         out_shape=jax.ShapeDtypeStruct((chans, samples), jnp.bfloat16),
-        in_specs=[pl.BlockSpec(memory_space=pl.ANY), vmem, vmem],
+        in_specs=[pl.BlockSpec(memory_space=pl.ANY)] * 3,
         out_specs=vmem,
         scratch_shapes=[
+            pltpu.VMEM((1, 2 * BLOCK), jnp.float32),
+            pltpu.VMEM((RANK, WIN), jnp.float32),
+            pltpu.SemaphoreType.DMA((2,)),
             pltpu.VMEM((672, samples + 2 * EDGE), jnp.bfloat16),
             pltpu.VMEM((640, samples), jnp.bfloat16),
             pltpu.VMEM((2 * BLOCK, BLOCK), jnp.bfloat16),
@@ -389,7 +423,7 @@
             pltpu.SemaphoreType.DMA((2,)),
         ],
         compiler_params=pltpu.CompilerParams(
-            collective_id=0, has_side_effects=True, vmem_limit_bytes=48 * 1024 * 1024
+            collective_id=0, has_side_effects=True, vmem_limit_bytes=60 * 1024 * 1024
         ),
     )(raw, taps, start_basis.T)
 

time: 88 us -> 86.8 us (0.986)
  Pallas kernels: 83.1 us -> 82 us
    pallas_call x1, Pallas kernels: 83.1 us -> 82 us  [per_device(): pl.pallas_call(functools.partial(kernel, nch, nta), out_shape=jax.ShapeDt...]
    unnamed x5 -> x1, local copies, waits for them, and re-layouts: 3.99 us -> 3.4 us
where the time goes in v3:
time: 86.8 us; the launch traced here: 86.6 us
  Pallas kernels  82 us (94%)
  local copies, waits for them, and re-layouts  3.4 us (4%)
  other arithmetic  1.23 us (1%)
    pallas_call x1, Pallas kernels, per_device(): pl.pallas_call(functools.partial(kernel, nch, nta), out_shape=jax.ShapeDt...  82 us
    unnamed x1, local copies, waits for them, and re-layouts  3.4 us

profile of v3, /device:TPU:4, one launch (start us, length us, event | category | flops | bytes accessed | tf_op | source)
XLA Modules:
  0.0 86.6 jit_solution(8287744759419247229)
XLA Ops:
  0.0 1.2 %pad_convert_fusion = f32[512]{0:T(512)} fusion(bf16[129]{0:T(256)(128)(2,1)} %param.4), kind=kLoop, calls=%fused_computation | loop fusion | flops 512 | bytes 2306 | tf_op jit(solution)/shard_map/broadcast_in_dim | solution.py:398
  1.2 82.0 %shard_map.37 = bf16[256,5120]{1,0:T(8,128)(2,1)} custom-call(bf16[256,5120]{1,0:T(8,128)(2,1)} %raw.1, f32[1,512]{1,0:T(1,128)} %bitcast.3, f32[16,512]{1,0:T(8,128)} %bitcast.2), custom_call_target="tpu_custom_call" | custom-call | tf_op jit(solution)/shard_map/pallas_call | solution.py:400
  83.2 3.4 %copy.5 = bf16[256,5120]{1,0:T(8,128)(2,1)} copy(bf16[256,5120]{1,0:T(8,128)(2,1)} %shard_map.37) | data formatting | bytes 5242880

commit v4 on v3

--- a/solution.py
+++ b/solution.py
@@ -93,6 +93,7 @@
 def kernel(
     nch, nta, raw, taps_in, start_in, out,
     taps, start, small_sem, x, gz, band, part, recv, s_hi, s_lo, basis,
+    hold, top, leg_sem, top_sem,
     own_sem, halo_send, halo_recv, part_send, part_recv, basis_send, basis_recv,
 ):
     c = lax.axis_index("ch")
@@ -104,7 +105,7 @@
     def exists(dc, dt):
         return (c + dc >= 0) & (c + dc < nch) & (t + dt >= 0) & (t + dt < nta)
 
-    partners = [(dc, dt) for dc in (-2, -1, 0, 1, 2) for dt in (-1, 0, 1) if (dc, dt) != (0, 0)]
+    partners = [(dc, dt) for dc in (-1, 0, 1) for dt in (-1, 0, 1) if (dc, dt) != (0, 0)]
     partners += [(0, dt) for dt in range(1 - nta, nta) if abs(dt) > 1]
 
     own = pltpu.make_async_copy(raw, x.at[272:528, EDGE:right], own_sem)
@@ -119,9 +120,17 @@
         @pl.when(exists(dc, dt))
         def _():
             pl.semaphore_signal(barrier, inc=1, device_id=(c + dc, t + dt), device_id_type=MESH)
-    near = 1 + sum(((c + dc >= 0) & (c + dc < nch)).astype(jnp.int32) for dc in (-2, -1, 1, 2))
+    near = 1 + sum(((c + dc >= 0) & (c + dc < nch)).astype(jnp.int32) for dc in (-1, 1))
     around = 1 + sum(((t + dt >= 0) & (t + dt < nta)).astype(jnp.int32) for dt in (-1, 1))
-    pl.semaphore_wait(barrier, near * around - 1 + nta - around)
+    count = near * around - 1 + nta - around
+    if nch == 8:
+        turning = (c % 4 == 0) | (c % 4 == 3)
+        @pl.when(turning)
+        def _():
+            for other in ((c + 4) % 8, jnp.where(c < 4, 3 - c, 11 - c)):
+                pl.semaphore_signal(barrier, inc=1, device_id=(other, t), device_id_type=MESH)
+        count = count + jnp.where(turning, 2, 0)
+    pl.semaphore_wait(barrier, count)
 
     mid = (EDGE, right)
     whole = (0, samples)
@@ -136,13 +145,12 @@
         (1, -1, (0, 256), head, (16, 272), high),
         (-1, 1, (0, 144), tail, (528, 672), low),
         (-1, -1, (0, 144), head, (528, 672), high),
-        (2, 0, (240, 256), whole, (0, 16), mid),
-        (2, 1, (240, 256), tail, (0, 16), low),
-        (2, -1, (240, 256), head, (0, 16), high),
         (1, 0, (112, 240), whole, (128, 256), mid),
-        (-1, 0, (16, 144), whole, (544, 672), mid),
+        (-1, 0, (16, 80), whole, (544, 608), mid),
+        (-1, 0, (80, 144), whole, (608, 672), mid),
         (1, 0, (0, 112), whole, (16, 128), mid),
     ]
+    detours = [(11, 3, 7, 4), (10, 4, 0, 3)] if nch == 8 else []
 
     def halo(index):
         dc, dt, rows, cols, to_rows, to_cols = kinds[index]
@@ -155,15 +163,70 @@
             device_id_type=MESH,
         )
 
+    def first_leg(index, by):
+        rows = kinds[index][2]
+        return pltpu.make_async_remote_copy(
+            src_ref=raw.at[rows[0] : rows[1]],
+            dst_ref=hold.at[0 : rows[1] - rows[0]],
+            send_sem=leg_sem.at[0],
+            recv_sem=leg_sem.at[1],
+            device_id=(by, t),
+            device_id_type=MESH,
+        )
+
+    def second_leg(index, to):
+        rows, _, to_rows, to_cols = kinds[index][2:]
+        return pltpu.make_async_remote_copy(
+            src_ref=hold.at[0 : rows[1] - rows[0]],
+            dst_ref=x.at[to_rows[0] : to_rows[1], to_cols[0] : to_cols[1]],
+            send_sem=leg_sem.at[2],
+            recv_sem=halo_recv.at[index],
+            device_id=(to, t),
+            device_id_type=MESH,
+        )
+
     def each_halo(indices, sign, act):
         for index in indices:
             dc, dt = kinds[index][:2]
-            @pl.when(exists(sign * dc, sign * dt))
+            wanted = exists(sign * dc, sign * dt)
+            if sign > 0:
+                for number, source, _, _ in detours:
+                    if number == index:
+                        wanted = wanted & (c != source)
+            @pl.when(wanted)
             def _():
                 act(halo(index))
 
     everything = range(len(kinds))
-    each_halo(everything, 1, lambda copy: copy.start())
+    each_halo(range(0, 8), 1, lambda copy: copy.start())
+    for index, source, by, _ in detours:
+        @pl.when(c == source)
+        def _():
+            first_leg(index, by).start()
+    each_halo(range(8, 12), 1, lambda copy: copy.start())
+
+    @pl.when(t == 0)
+    def _():
+        x[16:672, 0:EDGE] = jnp.zeros((656, EDGE), x.dtype)
+
+    @pl.when(t == nta - 1)
+    def _():
+        x[16:672, right : right + EDGE] = jnp.zeros((656, EDGE), x.dtype)
+
+    @pl.when(c == 0)
+    def _():
+        x[256:272, :] = jnp.zeros((16, x.shape[1]), x.dtype)
+
+    x[0:16, :] = jnp.zeros((16, x.shape[1]), x.dtype)
+
+    @pl.when(c == nch - 1)
+    def _():
+        x[528:544, :] = jnp.zeros((16, x.shape[1]), x.dtype)
+        gz[512:640, :] = jnp.zeros((STRIDE, samples), gz.dtype)
+
+    @pl.when(c == 0)
+    def _():
+        gz[256:512, :] = jnp.zeros((2 * STRIDE, samples), gz.dtype)
 
     taps_copy.wait()
     start_copy.wait()
@@ -257,11 +320,22 @@
     own.wait()
     each_halo(range(0, 8), -1, lambda copy: copy.wait_recv())
     gauge(2, 2)
+    top_copy = pltpu.make_async_remote_copy(
+        src_ref=gz.at[0:16],
+        dst_ref=top,
+        send_sem=top_sem.at[0],
+        recv_sem=top_sem.at[1],
+        device_id=(c + 1, t),
+        device_id_type=MESH,
+    )
+    @pl.when(c < nch - 1)
+    def _():
+        top_copy.start()
     products([((0, 256), 0, 0), ((128, 256), 128, 256)])
     send_part("own", 0)
     send_part("own", 1)
 
-    each_halo([11], -1, lambda copy: copy.wait_recv())
+    each_halo([8], -1, lambda copy: copy.wait_recv())
     @pl.when(c > 0)
     def _():
         gauge(1, 1)
@@ -270,7 +344,7 @@
     send_part("next", 1)
 
     def tile_after():
-        each_halo([12], -1, lambda copy: copy.wait_recv())
+        each_halo([9, 10], -1, lambda copy: copy.wait_recv())
         @pl.when(c < nch - 1)
         def _():
             gauge(4, 1)
@@ -278,12 +352,20 @@
         send_part("far", 1)
 
     def first_tile():
-        each_halo([8, 9, 10, 13], -1, lambda copy: copy.wait_recv())
+        each_halo([11], -1, lambda copy: copy.wait_recv())
         @pl.when(c > 0)
         def _():
             gauge(0, 1)
+            top_copy.wait_recv()
+            gz[384:400, :] = top[...]
         products([((0, 512), 384, 1280)])
         send_part("far", 0)
+
+    for index, _, by, to in detours:
+        @pl.when(c == by)
+        def _():
+            first_leg(index, by).wait_recv()
+            second_leg(index, to).start()
 
     @pl.when(c % 2 == 1)
     def _():
@@ -381,6 +463,16 @@
         out[:, cols] = (gz[0:256, cols].astype(jnp.float32) - fitted).astype(out.dtype)
 
     each_halo(everything, 1, lambda copy: copy.wait_send())
+    @pl.when(c < nch - 1)
+    def _():
+        top_copy.wait_send()
+    for index, source, by, to in detours:
+        @pl.when(c == source)
+        def _():
+            first_leg(index, by).wait_send()
+        @pl.when(c == by)
+        def _():
+            second_leg(index, to).wait_send()
     for window in (0, 1):
         @pl.when(t != owners[window])
         def _():
@@ -414,9 +506,13 @@
             pltpu.VMEM((WIN, WIN), jnp.bfloat16),
             pltpu.VMEM((WIN, WIN), jnp.bfloat16),
             pltpu.VMEM((2, RANK, 640), jnp.bfloat16),
+            pltpu.VMEM((112, samples), jnp.bfloat16),
+            pltpu.VMEM((16, samples), jnp.bfloat16),
+            pltpu.SemaphoreType.DMA((3,)),
+            pltpu.SemaphoreType.DMA((2,)),
             pltpu.SemaphoreType.DMA,
-            pltpu.SemaphoreType.DMA((14,)),
-            pltpu.SemaphoreType.DMA((14,)),
+            pltpu.SemaphoreType.DMA((12,)),
+            pltpu.SemaphoreType.DMA((12,)),
             pltpu.SemaphoreType.DMA((2, 3)),
             pltpu.SemaphoreType.DMA((nta, 3)),
             pltpu.SemaphoreType.DMA((2, nta)),

time: 86.8 us -> 77.6 us (0.89)
  Pallas kernels: 82 us -> 72.8 us
    pallas_call x1, Pallas kernels: 82 us -> 72.8 us  [per_device(): pl.pallas_call(functools.partial(kernel, nch, nta), out_shape=jax.ShapeDt...]
where the time goes in v4:
time: 77.6 us; the launch traced here: 77.4 us
  Pallas kernels  72.8 us (94%)
  local copies, waits for them, and re-layouts  3.4 us (4%)
  other arithmetic  1.23 us (2%)
    pallas_call x1, Pallas kernels, per_device(): pl.pallas_call(functools.partial(kernel, nch, nta), out_shape=jax.ShapeDt...  72.8 us
    unnamed x1, local copies, waits for them, and re-layouts  3.4 us

profile of v4, /device:TPU:4, one launch (start us, length us, event | category | flops | bytes accessed | tf_op | source)
XLA Modules:
  0.0 77.4 jit_solution(9980034615571868728)
XLA Ops:
  0.0 1.2 %pad_convert_fusion = f32[512]{0:T(512)} fusion(bf16[129]{0:T(256)(128)(2,1)} %param.4), kind=kLoop, calls=%fused_computation | loop fusion | flops 512 | bytes 2306 | tf_op jit(solution)/shard_map/broadcast_in_dim | solution.py:490
  1.2 72.8 %shard_map.37 = bf16[256,5120]{1,0:T(8,128)(2,1)} custom-call(bf16[256,5120]{1,0:T(8,128)(2,1)} %raw.1, f32[1,512]{1,0:T(1,128)} %bitcast.3, f32[16,512]{1,0:T(8,128)} %bitcast.2), custom_call_target="tpu_custom_call" | custom-call | tf_op jit(solution)/shard_map/pallas_call | solution.py:492
  74.0 3.4 %copy.5 = bf16[256,5120]{1,0:T(8,128)(2,1)} copy(bf16[256,5120]{1,0:T(8,128)(2,1)} %shard_map.37) | data formatting | bytes 5242880

commit v5 on v4

--- a/solution.py
+++ b/solution.py
@@ -519,7 +519,7 @@
             pltpu.SemaphoreType.DMA((2,)),
         ],
         compiler_params=pltpu.CompilerParams(
-            collective_id=0, has_side_effects=True, vmem_limit_bytes=60 * 1024 * 1024
+            collective_id=0, has_side_effects=True, vmem_limit_bytes=50 * 1024 * 1024
         ),
     )(raw, taps, start_basis.T)
 

time: 77.6 us -> 74.4 us (0.959)
  Pallas kernels: 72.8 us -> 71.3 us
  local copies, waits for them, and re-layouts: 3.4 us -> 2.25 us
    pallas_call x1, Pallas kernels: 72.8 us -> 71.3 us  [per_device(): pl.pallas_call(functools.partial(kernel, nch, nta), out_shape=jax.ShapeDt...]
    unnamed x1 -> x3, local copies, waits for them, and re-layouts: 3.4 us -> 2.25 us
where the time goes in v5:
time: 74.4 us; the launch traced here: 74.2 us
  Pallas kernels  71.3 us (96%)
  local copies, waits for them, and re-layouts  2.25 us (3%)
    pallas_call x1, Pallas kernels, per_device(): pl.pallas_call(functools.partial(kernel, nch, nta), out_shape=jax.ShapeDt...  71.3 us
    unnamed x3, local copies, waits for them, and re-layouts  2.25 us

profile of v5, /device:TPU:4, one launch (start us, length us, event | category | flops | bytes accessed | tf_op | source)
XLA Modules:
  0.0 74.2 jit_solution(14356732230651074581)
XLA Ops:
  0.0 0.7 pad_convert_fusion
  0.7 0.0 copy-start
  0.7 0.8 %copy-done = f32[512,16]{0,1:T(8,128)S(1)} copy-done((f32[512,16]{0,1:T(8,128)S(1)}, f32[512,16]{0,1:T(8,128)}, u32[]{:S(2)}) %copy-start) | copy-done | bytes 32792
  1.4 71.3 %shard_map.37 = bf16[256,5120]{1,0:T(8,128)(2,1)S(1)} custom-call(bf16[256,5120]{1,0:T(8,128)(2,1)} %raw.1, f32[1,512]{1,0:T(1,128)S(1)} %bitcast.3, f32[16,512]{1,0:T(8,128)S(1)} %bitcast.2), custom_call_target="tpu_custom_call" | custom-call | tf_op jit(solution)/shard_map/pallas_call | solution.py:492
  72.7 1.5 %copy.5 = bf16[256,5120]{1,0:T(8,128)(2,1)} copy(bf16[256,5120]{1,0:T(8,128)(2,1)S(1)} %shard_map.37) | data formatting | bytes 5242880
Async XLA Ops:
  0.7 0.8 %copy-start = (f32[512,16]{0,1:T(8,128)S(1)}, f32[512,16]{0,1:T(8,128)}, u32[]{:S(2)}) copy-start(f32[512,16]{0,1:T(8,128)} %param.5) | copy-start | bytes 98308
